TPU v7x, 128 devices: a whole 4x4x4 slice. The times are simulated.
128 devices in a mesh: replica: 16 (over z_hi, y, core), shard: 8 (over x, z_lo).
Axes of the slice: x: 4, y: 4, z: 4 (z_hi: 2, z_lo: 2; z = z_hi * 2 + z_lo), core: 2. Of those that a mesh axis runs over, the one named last changes fastest.
Arguments:
- student_ctx: bfloat16 [163840, 1536], P(('replica', 'shard')), may hold values from -24 to 24
- out_grad: bfloat16 [163840, 1536], P(('replica', 'shard')), may hold values from -0.015625 to 0.015625
- weight: float32 [1536, 1536], P('shard'), may hold values from -0.15625 to 0.15625
- moment_one: float32 [1536, 1536], P('shard'), may hold values from -6 to 6
- moment_two: float32 [1536, 1536], P('shard'), may hold values from 0.05 to 2
- teacher: float32 [1536, 1536], P('shard'), may hold values from -0.15625 to 0.15625
- teach_input: bfloat16 [65536, 1536], P(('replica', 'shard')), may hold values from -6 to 6
- teach_ctx: bfloat16 [65536, 1536], P(('replica', 'shard')), may hold values from -6 to 6
Outputs:
- ctx_grad: bfloat16 [163840, 1536], P(('replica', 'shard'))
- weight_next: float32 [1536, 1536], P('shard')
- moment_one_next: float32 [1536, 1536], P('shard')
- moment_two_next: float32 [1536, 1536], P('shard')
- teacher_next: float32 [1536, 1536], P('shard')
- teacher_out: bfloat16 [65536, 1536], P(('replica', 'shard'))
All inputs are finite; a program needn't handle non-finite values.
Results may differ from a plain program's by a relative error of at most 0.0043.
The roundings to bfloat16 on the way count: a program that leaves them out, or rounds other values in their place, can miss the bound.
Values may be sent and summed in bfloat16 or wider, within the bound.
A program may use at most 192 MiB of HBM per device.

v0:
```python
import jax
import jax.numpy as jnp
from jax import lax
from jax.sharding import PartitionSpec as P

STEP = 100
beta_one = 0.9
beta_two = 0.999
adam_eps = 1e-08
learn_rate = 0.001
decay_rate = 0.04
momentum = 0.994


def body(student_ctx, out_grad, weight, moment_one, moment_two, teacher, teach_input, teach_ctx):
    features = weight.shape[1]
    token_count = student_ctx.shape[0]
    weight_half = weight.astype(jnp.bfloat16)
    teacher_next = momentum * teacher + (1.0 - momentum) * weight
    teacher_half = teacher_next.astype(jnp.bfloat16)
    columns = teach_ctx
    projected = jnp.dot(
        columns,
        lax.all_gather(teacher_half, "shard", axis=0, tiled=True),
        preferred_element_type=jnp.float32,
    )
    teacher_out = (teach_input.astype(jnp.float32) + projected).astype(jnp.bfloat16)
    product = lax.dot_general(
        out_grad,
        lax.all_gather(weight_half, "shard", axis=0, tiled=True),
        (((1,), (1,)), ((), ())),
        preferred_element_type=jnp.float32,
    )
    ctx_grad = product.astype(jnp.bfloat16)
    n_copies = lax.axis_size("replica")
    n_groups = lax.axis_size("shard")
    block_rows = features // (n_copies * n_groups)
    virtual_ctx = student_ctx.reshape(token_count, n_groups, n_copies, block_rows)
    virtual_ctx = virtual_ctx.transpose(0, 2, 1, 3).reshape(token_count, features)
    columns = virtual_ctx
    own_block = lax.psum_scatter(
        lax.dot_general(
            columns, out_grad, (((0,), (0,)), ((), ())), preferred_element_type=jnp.float32
        ),
        ("replica", "shard"),
        scatter_dimension=0,
        tiled=True,
    )
    gradient = lax.all_gather(own_block.astype(jnp.bfloat16), "replica", axis=0, tiled=True).astype(
        own_block.dtype
    )
    moment_one_next = beta_one * moment_one + (1.0 - beta_one) * gradient
    moment_two_next = beta_two * moment_two + (1.0 - beta_two) * gradient * gradient
    correct_one = 1.0 - beta_one**STEP
    correct_two = 1.0 - beta_two**STEP
    update = (
        moment_one_next / correct_one / (jnp.sqrt(moment_two_next / correct_two) + adam_eps)
        + decay_rate * weight
    )
    weight_next = weight - learn_rate * update
    return (ctx_grad, weight_next, moment_one_next, moment_two_next, teacher_next, teacher_out)


def solution(mesh):
    return jax.shard_map(
        body,
        mesh=mesh,
        in_specs=(
            P(("replica", "shard"), None),
            P(("replica", "shard"), None),
            P("shard", None),
            P("shard", None),
            P("shard", None),
            P("shard", None),
            P(("replica", "shard"), None),
            P(("replica", "shard"), None),
        ),
        out_specs=(
            P(("replica", "shard"), None),
            P("shard", None),
            P("shard", None),
            P("shard", None),
            P("shard", None),
            P(("replica", "shard"), None),
        ),
        check_vma=False,
    )
```

profile of v0, /device:TPU:4, one launch (start us, length us, event | category | flops | bytes accessed | tf_op | source)
XLA Modules:
  0.0 783.4 jit_solution(11342597224027583799)
XLA Ops:
  7.2 6.4 copy.20
  13.6 6.9 reshape.18
  20.5 5.5 copy.21
  26.0 7.0 reshape.19
  33.0 11.5 %fusion.8 = f32[1536,1536]{1,0:T(8,128)} fusion(bf16[1280,1536]{0,1:T(8,128)(2,1)} %reshape.19, bf16[1280,1536]{1,0:T(8,128)(2,1)} %param.9), kind=kOutput, calls=%fused_computation.13 | convolution fusion | flops 6039797760 | bytes 17301504 | tf_op jit(solution)/shard_map/dot_general | solution.py:42
  44.5 367.8 %fusion = f32[16,1536]{1,0:T(8,128)S(1)} fusion(f32[1536,1536]{1,0:T(8,128)} %fusion.8), kind=kCustom, calls=%all-reduce-scatter | all-reduce-scatter fusion | flops 3145729 | bytes 9535488
  416.2 14.3 %collective-permute-start.28 = (bf16[16,1536]{1,0:T(8,128)(2,1)S(1)}, bf16[16,1536]{1,0:T(8,128)(2,1)S(1)}, u32[]{:S(2)}, u32[]{:S(2)}) collective-permute-start(bf16[16,1536]{1,0:T(8,128)(2,1)S(1)} %convert.62), channel_id=1, source_target_pairs={{0,29},{1,30},{2,31},{3,32},{4,33},{5,34},{6,35},{7,36},{8,37},{9,... | collective-permute-start | bytes 147464
  438.4 8.7 %collective-permute-start.21 = (bf16[16,1536]{1,0:T(8,128)(2,1)S(1)}, bf16[16,1536]{1,0:T(8,128)(2,1)S(1)}, u32[]{:S(2)}, u32[]{:S(2)}) collective-permute-start(bf16[16,1536]{1,0:T(8,128)(2,1)S(1)} %convert.62), channel_id=1, source_target_pairs={{0,22},{1,23},{2,24},{3,25},{4,26},{5,27},{6,28},{7,29},{8,30},{9,... | collective-permute-start | bytes 147464
  447.1 4.8 collective-permute-start.20
  451.9 4.5 collective-permute-start.19
  463.8 3.5 collective-permute-start.14
  469.0 4.0 collective-permute-start.12
  478.1 3.6 collective-permute-start.9
  491.0 4.0 collective-permute-start.4
  497.0 4.2 collective-permute-start.2
  501.3 3.4 collective-permute-start.1
  508.4 3.2 collective-permute-done
  511.7 25.9 %concatenate = bf16[524,1536]{1,0:T(8,128)(2,1)S(1)} concatenate(bf16[12,1536]{1,0:T(8,128)(2,1)S(1)} %collective-permute-done.31, bf16[16,1536]{1,0:T(8,128)(2,1)S(1)} %collective-permute-done.30, bf16[16,1536]{1,0:T(8,128)(2,1)S(1)} %collective-permute-done.29, bf16[16,1536]{1,0:T(8,128)(2,1)S(1)} %collective-permute-done.28, bf16[16,1536]{1,0:T(8,128)(2,1)S(1)} %collective-permute-done.27, ...), dimensions={0} | concatenate | bytes 3268608
  537.7 21.4 %all-gather = bf16[16,12,1536]{2,1,0:T(8,128)(2,1)S(1)} all-gather(bf16[1,12,1536]{2,1,0:T(8,128)(2,1)S(1)} %fusion.4), channel_id=1, replica_groups=mesh['replica'=16,'shard'=8] {'replica'}, dimensions={0}, use_global_device_ids=true | all-gather | bytes 626688 | tf_op jit(solution)/shard_map/all_gather | solution.py:49
  559.2 5.6 fusion.5
  567.3 96.4 %all-gather.6.cloned.1.call-done = bf16[1536,1536]{1,0:T(8,128)(2,1)} async-done(((bf16[192,1536]{1,0:T(8,128)(2,1)}), bf16[1536,1536]{1,0:T(8,128)(2,1)}) %all-gather.6.cloned.1.call-update) | async-done | bytes 4718608 | tf_op jit(solution)/shard_map/all_gather | solution.py:24
  663.7 6.1 fusion.2
  672.4 93.5 %all-gather.4.cloned.1.call-done = bf16[1536,1536]{1,0:T(8,128)(2,1)} async-done(((bf16[192,1536]{1,0:T(8,128)(2,1)}), bf16[1536,1536]{1,0:T(8,128)(2,1)}) %all-gather.4.cloned.1.call-update) | async-done | bytes 4718608 | tf_op jit(solution)/shard_map/all_gather | solution.py:30
  765.9 10.6 %convolution_convert_fusion = bf16[1280,1536]{1,0:T(8,128)(2,1)} fusion(bf16[1280,1536]{1,0:T(8,128)(2,1)} %param.9, bf16[1536,1536]{1,0:T(8,128)(2,1)} %all-gather.4.cloned.1.call-done), kind=kOutput, calls=%fused_computation | convolution fusion | flops 6041763840 | bytes 12582912 | tf_op jit(solution)/shard_map/dot_general | solution.py:28
  (117 shorter events, 45.5 us)
Async XLA Ops:
  7.2 656.5 %all-gather.6.cloned.1.call-start = ((), (), s32[]{:S(2)}) async-start(), calls=%async_computation.1 | async-start | bytes 5308416 | tf_op jit(solution)/shard_map/all_gather | solution.py:24
  412.3 20.8 %collective-permute-start.30 = (bf16[16,1536]{1,0:T(8,128)(2,1)S(1)}, bf16[16,1536]{1,0:T(8,128)(2,1)S(1)}, u32[]{:S(2)}, u32[]{:S(2)}) collective-permute-start(bf16[16,1536]{1,0:T(8,128)(2,1)S(1)} %convert.62), channel_id=1, source_target_pairs={{0,31},{1,32},{2,33},{3,34},{4,35},{5,36},{6,37},{7,38},{8,39},{9,... | collective-permute-start | bytes 147464
  413.6 18.2 %collective-permute-start.31 = (bf16[12,1536]{1,0:T(8,128)(2,1)S(1)}, bf16[12,1536]{1,0:T(8,128)(2,1)S(1)}, u32[]{:S(2)}, u32[]{:S(2)}) collective-permute-start(bf16[12,1536]{1,0:T(8,128)(2,1)S(1)} %slice), channel_id=1, source_target_pairs={{0,32},{1,33},{2,34},{3,35},{4,36},{5,37},{6,38},{7,39},{8,40},{9,... | collective-permute-start | bytes 110600
  414.9 19.5 %collective-permute-start.29 = (bf16[16,1536]{1,0:T(8,128)(2,1)S(1)}, bf16[16,1536]{1,0:T(8,128)(2,1)S(1)}, u32[]{:S(2)}, u32[]{:S(2)}) collective-permute-start(bf16[16,1536]{1,0:T(8,128)(2,1)S(1)} %convert.62), channel_id=1, source_target_pairs={{0,30},{1,31},{2,32},{3,33},{4,34},{5,35},{6,36},{7,37},{8,38},{9,... | collective-permute-start | bytes 147464
  416.2 19.5 %collective-permute-start.28 = (bf16[16,1536]{1,0:T(8,128)(2,1)S(1)}, bf16[16,1536]{1,0:T(8,128)(2,1)S(1)}, u32[]{:S(2)}, u32[]{:S(2)}) collective-permute-start(bf16[16,1536]{1,0:T(8,128)(2,1)S(1)} %convert.62), channel_id=1, source_target_pairs={{0,29},{1,30},{2,31},{3,32},{4,33},{5,34},{6,35},{7,36},{8,37},{9,... | collective-permute-start | bytes 147464
  433.1 13.9 %collective-permute-start.25 = (bf16[16,1536]{1,0:T(8,128)(2,1)S(1)}, bf16[16,1536]{1,0:T(8,128)(2,1)S(1)}, u32[]{:S(2)}, u32[]{:S(2)}) collective-permute-start(bf16[16,1536]{1,0:T(8,128)(2,1)S(1)} %convert.62), channel_id=1, source_target_pairs={{0,26},{1,27},{2,28},{3,29},{4,30},{5,31},{6,32},{7,33},{8,34},{9,... | collective-permute-start | bytes 147464
  434.5 17.4 %collective-permute-start.24 = (bf16[16,1536]{1,0:T(8,128)(2,1)S(1)}, bf16[16,1536]{1,0:T(8,128)(2,1)S(1)}, u32[]{:S(2)}, u32[]{:S(2)}) collective-permute-start(bf16[16,1536]{1,0:T(8,128)(2,1)S(1)} %convert.62), channel_id=1, source_target_pairs={{0,25},{1,26},{2,27},{3,28},{4,29},{5,30},{6,31},{7,32},{8,33},{9,... | collective-permute-start | bytes 147464
  435.8 20.7 %collective-permute-start.23 = (bf16[16,1536]{1,0:T(8,128)(2,1)S(1)}, bf16[16,1536]{1,0:T(8,128)(2,1)S(1)}, u32[]{:S(2)}, u32[]{:S(2)}) collective-permute-start(bf16[16,1536]{1,0:T(8,128)(2,1)S(1)} %convert.62), channel_id=1, source_target_pairs={{0,24},{1,25},{2,26},{3,27},{4,28},{5,29},{6,30},{7,31},{8,32},{9,... | collective-permute-start | bytes 147464
  437.1 20.9 %collective-permute-start.22 = (bf16[16,1536]{1,0:T(8,128)(2,1)S(1)}, bf16[16,1536]{1,0:T(8,128)(2,1)S(1)}, u32[]{:S(2)}, u32[]{:S(2)}) collective-permute-start(bf16[16,1536]{1,0:T(8,128)(2,1)S(1)} %convert.62), channel_id=1, source_target_pairs={{0,23},{1,24},{2,25},{3,26},{4,27},{5,28},{6,29},{7,30},{8,31},{9,... | collective-permute-start | bytes 147464
  438.4 21.8 %collective-permute-start.21 = (bf16[16,1536]{1,0:T(8,128)(2,1)S(1)}, bf16[16,1536]{1,0:T(8,128)(2,1)S(1)}, u32[]{:S(2)}, u32[]{:S(2)}) collective-permute-start(bf16[16,1536]{1,0:T(8,128)(2,1)S(1)} %convert.62), channel_id=1, source_target_pairs={{0,22},{1,23},{2,24},{3,25},{4,26},{5,27},{6,28},{7,29},{8,30},{9,... | collective-permute-start | bytes 147464
  447.1 14.4 %collective-permute-start.20 = (bf16[16,1536]{1,0:T(8,128)(2,1)S(1)}, bf16[16,1536]{1,0:T(8,128)(2,1)S(1)}, u32[]{:S(2)}, u32[]{:S(2)}) collective-permute-start(bf16[16,1536]{1,0:T(8,128)(2,1)S(1)} %convert.62), channel_id=1, source_target_pairs={{0,21},{1,22},{2,23},{3,24},{4,25},{5,26},{6,27},{7,28},{8,29},{9,... | collective-permute-start | bytes 147464
  460.2 12.8 %collective-permute-start.16 = (bf16[16,1536]{1,0:T(8,128)(2,1)S(1)}, bf16[16,1536]{1,0:T(8,128)(2,1)S(1)}, u32[]{:S(2)}, u32[]{:S(2)}) collective-permute-start(bf16[16,1536]{1,0:T(8,128)(2,1)S(1)} %convert.62), channel_id=1, source_target_pairs={{0,17},{1,18},{2,19},{3,20},{4,21},{5,22},{6,23},{7,24},{8,25},{9,... | collective-permute-start | bytes 147464
  461.6 13.7 %collective-permute-start.15 = (bf16[16,1536]{1,0:T(8,128)(2,1)S(1)}, bf16[16,1536]{1,0:T(8,128)(2,1)S(1)}, u32[]{:S(2)}, u32[]{:S(2)}) collective-permute-start(bf16[16,1536]{1,0:T(8,128)(2,1)S(1)} %convert.62), channel_id=1, source_target_pairs={{0,16},{1,17},{2,18},{3,19},{4,20},{5,21},{6,22},{7,23},{8,24},{9,... | collective-permute-start | bytes 147464
  463.8 14.3 %collective-permute-start.14 = (bf16[16,1536]{1,0:T(8,128)(2,1)S(1)}, bf16[16,1536]{1,0:T(8,128)(2,1)S(1)}, u32[]{:S(2)}, u32[]{:S(2)}) collective-permute-start(bf16[16,1536]{1,0:T(8,128)(2,1)S(1)} %convert.62), channel_id=1, source_target_pairs={{0,15},{1,16},{2,17},{3,18},{4,19},{5,20},{6,21},{7,22},{8,23},{9,... | collective-permute-start | bytes 147464
  467.3 14.4 %collective-permute-start.13 = (bf16[16,1536]{1,0:T(8,128)(2,1)S(1)}, bf16[16,1536]{1,0:T(8,128)(2,1)S(1)}, u32[]{:S(2)}, u32[]{:S(2)}) collective-permute-start(bf16[16,1536]{1,0:T(8,128)(2,1)S(1)} %convert.62), channel_id=1, source_target_pairs={{0,14},{1,15},{2,16},{3,17},{4,18},{5,19},{6,20},{7,21},{8,22},{9,... | collective-permute-start | bytes 147464
  469.0 14.1 %collective-permute-start.12 = (bf16[16,1536]{1,0:T(8,128)(2,1)S(1)}, bf16[16,1536]{1,0:T(8,128)(2,1)S(1)}, u32[]{:S(2)}, u32[]{:S(2)}) collective-permute-start(bf16[16,1536]{1,0:T(8,128)(2,1)S(1)} %convert.62), channel_id=1, source_target_pairs={{0,13},{1,14},{2,15},{3,16},{4,17},{5,18},{6,19},{7,20},{8,21},{9,... | collective-permute-start | bytes 147464
  475.3 13.0 %collective-permute-start.10 = (bf16[16,1536]{1,0:T(8,128)(2,1)S(1)}, bf16[16,1536]{1,0:T(8,128)(2,1)S(1)}, u32[]{:S(2)}, u32[]{:S(2)}) collective-permute-start(bf16[16,1536]{1,0:T(8,128)(2,1)S(1)} %convert.62), channel_id=1, source_target_pairs={{0,11},{1,12},{2,13},{3,14},{4,15},{5,16},{6,17},{7,18},{8,19},{9,... | collective-permute-start | bytes 147464
  478.1 12.9 %collective-permute-start.9 = (bf16[16,1536]{1,0:T(8,128)(2,1)S(1)}, bf16[16,1536]{1,0:T(8,128)(2,1)S(1)}, u32[]{:S(2)}, u32[]{:S(2)}) collective-permute-start(bf16[16,1536]{1,0:T(8,128)(2,1)S(1)} %convert.62), channel_id=1, source_target_pairs={{0,10},{1,11},{2,12},{3,13},{4,14},{5,15},{6,16},{7,17},{8,18},{9,... | collective-permute-start | bytes 147464
  481.7 13.3 %collective-permute-start.8 = (bf16[16,1536]{1,0:T(8,128)(2,1)S(1)}, bf16[16,1536]{1,0:T(8,128)(2,1)S(1)}, u32[]{:S(2)}, u32[]{:S(2)}) collective-permute-start(bf16[16,1536]{1,0:T(8,128)(2,1)S(1)} %convert.62), channel_id=1, source_target_pairs={{0,9},{1,10},{2,11},{3,12},{4,13},{5,14},{6,15},{7,16},{8,17},{9,1... | collective-permute-start | bytes 147464
  483.2 13.8 %collective-permute-start.7 = (bf16[16,1536]{1,0:T(8,128)(2,1)S(1)}, bf16[16,1536]{1,0:T(8,128)(2,1)S(1)}, u32[]{:S(2)}, u32[]{:S(2)}) collective-permute-start(bf16[16,1536]{1,0:T(8,128)(2,1)S(1)} %convert.62), channel_id=1, source_target_pairs={{0,8},{1,9},{2,10},{3,11},{4,12},{5,13},{6,14},{7,15},{8,16},{9,17... | collective-permute-start | bytes 147464
  485.7 15.5 %collective-permute-start.6 = (bf16[16,1536]{1,0:T(8,128)(2,1)S(1)}, bf16[16,1536]{1,0:T(8,128)(2,1)S(1)}, u32[]{:S(2)}, u32[]{:S(2)}) collective-permute-start(bf16[16,1536]{1,0:T(8,128)(2,1)S(1)} %convert.62), channel_id=1, source_target_pairs={{0,7},{1,8},{2,9},{3,10},{4,11},{5,12},{6,13},{7,14},{8,15},{9,16}... | collective-permute-start | bytes 147464
  488.3 16.4 %collective-permute-start.5 = (bf16[16,1536]{1,0:T(8,128)(2,1)S(1)}, bf16[16,1536]{1,0:T(8,128)(2,1)S(1)}, u32[]{:S(2)}, u32[]{:S(2)}) collective-permute-start(bf16[16,1536]{1,0:T(8,128)(2,1)S(1)} %convert.62), channel_id=1, source_target_pairs={{0,6},{1,7},{2,8},{3,9},{4,10},{5,11},{6,12},{7,13},{8,14},{9,15},... | collective-permute-start | bytes 147464
  491.0 16.2 %collective-permute-start.4 = (bf16[16,1536]{1,0:T(8,128)(2,1)S(1)}, bf16[16,1536]{1,0:T(8,128)(2,1)S(1)}, u32[]{:S(2)}, u32[]{:S(2)}) collective-permute-start(bf16[16,1536]{1,0:T(8,128)(2,1)S(1)} %convert.62), channel_id=1, source_target_pairs={{0,5},{1,6},{2,7},{3,8},{4,9},{5,10},{6,11},{7,12},{8,13},{9,14},{... | collective-permute-start | bytes 147464
  564.8 201.1 %all-gather.4.cloned.1.call-start = ((), (), s32[]{:S(2)}) async-start(), calls=%async_computation | async-start | bytes 5308416 | tf_op jit(solution)/shard_map/all_gather | solution.py:30
  (37 other events, 1487.3 us)
Sparse Core Ops, SparseCore 0:
  564.9 98.6 all-gather.5
  665.3 100.5 all-gather.3
where the time goes:
time: 786 us; the launch traced here: 783 us
  blocking collectives  389 us (49%)
  waiting for transfers between devices  194 us (25%)
  starting transfers between devices  94.3 us (12%)
  local copies, waits for them, and re-layouts  57.3 us (7%)
  matrix products  28.3 us (4%)
  between operations  15 us (2%)
    unnamed x1, blocking collectives  368 us
    all_gather x1, waiting for transfers between devices, body(): lax.all_gather(teacher_half, 'shard', axis=0, tiled=True)  96.4 us
    unnamed x32, starting transfers between devices  94.1 us
    all_gather x1, waiting for transfers between devices, body(): lax.all_gather(weight_half, 'shard', axis=0, tiled=True)  93.5 us
    unnamed x60, local copies, waits for them, and re-layouts  37.8 us
    all_gather x1, blocking collectives, body(): lax.all_gather(own_block.astype(jnp.bfloat16), 'replica', axis=0, tiled=T...  21.4 us
  transfers between devices with their start and end apart: 34, of which 3 were waited for; matrix products, arithmetic and copies ran while one was open for 1% of the time, Pallas kernels for 0%

commit v1 on v0

--- a/solution.py
+++ b/solution.py
@@ -2,6 +2,7 @@
 import jax.numpy as jnp
 from jax import lax
 from jax.sharding import PartitionSpec as P
+from jax.lax import all_to_all, axis_size
 
 STEP = 100
 beta_one = 0.9
@@ -19,11 +20,10 @@
     teacher_next = momentum * teacher + (1.0 - momentum) * weight
     teacher_half = teacher_next.astype(jnp.bfloat16)
     columns = teach_ctx
-    projected = jnp.dot(
-        columns,
-        lax.all_gather(teacher_half, "shard", axis=0, tiled=True),
-        preferred_element_type=jnp.float32,
+    lay_the_scenes = lambda z_in: jnp.concatenate(
+        all_to_all(jnp.stack([z_in for _ in range(axis_size("shard"))]), "shard", 0, 0), 0
     )
+    projected = jnp.dot(columns, lay_the_scenes(teacher_half), preferred_element_type=jnp.float32)
     teacher_out = (teach_input.astype(jnp.float32) + projected).astype(jnp.bfloat16)
     product = lax.dot_general(
         out_grad,

time: 786 us -> 733 us (0.933)
  waiting for transfers between devices: 194 us -> 133 us
    all_gather x1 -> x0, waiting for transfers between devices: 96.4 us -> none  [body(): lax.all_gather(teacher_half, 'shard', axis=0, tiled=True)]
    all_to_all x0 -> x1, waiting for transfers between devices: none -> 75.6 us  [body(): all_to_all(jnp.stack([z_in for _ in range(axis_size('shard'))]), 'shard',...]
    all_gather x1, waiting for transfers between devices: 93.5 us -> 55.2 us  [body(): lax.all_gather(weight_half, 'shard', axis=0, tiled=True)]
    all_to_all x0 -> x1, starting transfers between devices: none -> 7.96 us  [body(): all_to_all(jnp.stack([z_in for _ in range(axis_size('shard'))]), 'shard',...]
    unnamed x60 -> x62, local copies, waits for them, and re-layouts: 37.8 us -> 36.6 us
  transfers between devices with their start and end apart: 34 -> 34, of which waited for: 3 -> 3; matrix products, arithmetic and copies ran while one was open for 1% -> 2% of each run, Pallas kernels for 0% -> 0%
where the time goes in v1:
time: 733 us; the launch traced here: 730 us
  blocking collectives  391 us (53%)
  waiting for transfers between devices  133 us (18%)
  starting transfers between devices  99.4 us (14%)
  local copies, waits for them, and re-layouts  58.7 us (8%)
  matrix products  27.7 us (4%)
  between operations  14.9 us (2%)
    unnamed x1, blocking collectives  368 us
    unnamed x32, starting transfers between devices  91.4 us
    all_to_all x1, waiting for transfers between devices, body(): all_to_all(jnp.stack([z_in for _ in range(axis_size('shard'))]), 'shard',...  75.6 us
    all_gather x1, waiting for transfers between devices, body(): lax.all_gather(weight_half, 'shard', axis=0, tiled=True)  55.2 us
    unnamed x62, local copies, waits for them, and re-layouts  36.6 us
    all_gather x1, blocking collectives, body(): lax.all_gather(own_block.astype(jnp.bfloat16), 'replica', axis=0, tiled=T...  22.5 us
  transfers between devices with their start and end apart: 34, of which 3 were waited for; matrix products, arithmetic and copies ran while one was open for 2% of the time, Pallas kernels for 0%

profile of v1, /device:TPU:4, one launch (start us, length us, event | category | flops | bytes accessed | tf_op | source)
XLA Modules:
  0.0 729.9 jit_solution(10619389782958326323)
XLA Ops:
  7.2 6.4 copy.20
  13.6 6.9 reshape.23
  20.5 5.5 copy.21
  26.0 7.0 reshape.24
  33.0 11.5 %fusion.8 = f32[1536,1536]{1,0:T(8,128)} fusion(bf16[1280,1536]{0,1:T(8,128)(2,1)} %reshape.24, bf16[1280,1536]{1,0:T(8,128)(2,1)} %param.9), kind=kOutput, calls=%fused_computation.13 | convolution fusion | flops 6039797760 | bytes 17301504 | tf_op jit(solution)/shard_map/dot_general | solution.py:42
  44.5 368.4 %fusion = f32[16,1536]{1,0:T(8,128)S(1)} fusion(f32[1536,1536]{1,0:T(8,128)} %fusion.8), kind=kCustom, calls=%all-reduce-scatter | all-reduce-scatter fusion | flops 3145729 | bytes 9535488
  425.0 12.1 %collective-permute-start.14 = (bf16[16,1536]{1,0:T(8,128)(2,1)S(1)}, bf16[16,1536]{1,0:T(8,128)(2,1)S(1)}, u32[]{:S(2)}, u32[]{:S(2)}) collective-permute-start(bf16[16,1536]{1,0:T(8,128)(2,1)S(1)} %convert.62), channel_id=1, source_target_pairs={{0,15},{1,16},{2,17},{3,18},{4,19},{5,20},{6,21},{7,22},{8,23},{9,... | collective-permute-start | bytes 147464
  438.4 8.0 %collective-permute-start.16 = (bf16[16,1536]{1,0:T(8,128)(2,1)S(1)}, bf16[16,1536]{1,0:T(8,128)(2,1)S(1)}, u32[]{:S(2)}, u32[]{:S(2)}) collective-permute-start(bf16[16,1536]{1,0:T(8,128)(2,1)S(1)} %convert.62), channel_id=1, source_target_pairs={{0,17},{1,18},{2,19},{3,20},{4,21},{5,22},{6,23},{7,24},{8,25},{9,... | collective-permute-start | bytes 147464
  446.4 7.2 collective-permute-start.17
  453.7 4.0 collective-permute-start.18
  461.3 3.0 collective-permute-start.20
  464.4 3.8 collective-permute-start.21
  479.9 3.2 collective-permute-start.28
  484.4 4.1 collective-permute-start.3
  497.5 4.3 collective-permute-start.7
  503.3 3.4 collective-permute-start.9
  508.1 26.0 %concatenate = bf16[524,1536]{1,0:T(8,128)(2,1)S(1)} concatenate(bf16[12,1536]{1,0:T(8,128)(2,1)S(1)} %collective-permute-done.31, bf16[16,1536]{1,0:T(8,128)(2,1)} %copy-done.22, bf16[16,1536]{1,0:T(8,128)(2,1)} %copy-done.20, bf16[16,1536]{1,0:T(8,128)(2,1)} %copy-done.19, bf16[16,1536]{1,0:T(8,128)(2,1)} %copy-done.18, bf16[16,1536]{1,0:T(8,128)(2,1)} %copy-done.17, ...), dimensions={0} | concatenate | bytes 3268608
  534.0 22.5 %all-gather = bf16[16,12,1536]{2,1,0:T(8,128)(2,1)S(1)} all-gather(bf16[1,12,1536]{2,1,0:T(8,128)(2,1)S(1)} %fusion.4), channel_id=1, replica_groups=mesh['replica'=16,'shard'=8] {'replica'}, dimensions={0}, use_global_device_ids=true | all-gather | bytes 626688 | tf_op jit(solution)/shard_map/all_gather | solution.py:49
  556.7 5.7 fusion.5
  565.0 8.0 %all-to-all-start = ((bf16[8,192,1536]{2,1,0:T(8,128)(2,1)}), bf16[8,192,1536]{2,1,0:T(8,128)(2,1)}, u32[]{:S(2)}, u32[]{:S(2)}) async-start(bf16[8,192,1536]{2,1,0:T(8,128)(2,1)} %stack.2), calls=%async_computation | async-start | bytes 9437184 | tf_op jit(solution)/shard_map/all_to_all | solution.py:24
  574.6 75.6 %all-to-all-done = bf16[8,192,1536]{2,1,0:T(8,128)(2,1)} async-done(((bf16[8,192,1536]{2,1,0:T(8,128)(2,1)}), bf16[8,192,1536]{2,1,0:T(8,128)(2,1)}, u32[]{:S(2)}, u32[]{:S(2)}) %all-to-all-start) | async-done | bytes 4718624 | tf_op jit(solution)/shard_map/all_to_all | solution.py:24
  650.2 5.5 fusion.2
  657.3 55.2 %all-gather.3.cloned.1.call-done = bf16[1536,1536]{1,0:T(8,128)(2,1)} async-done(((bf16[192,1536]{1,0:T(8,128)(2,1)}), bf16[1536,1536]{1,0:T(8,128)(2,1)}) %all-gather.3.cloned.1.call-update) | async-done | bytes 4718608 | tf_op jit(solution)/shard_map/all_gather | solution.py:30
  712.5 10.6 %convolution_convert_fusion = bf16[1280,1536]{1,0:T(8,128)(2,1)} fusion(bf16[1280,1536]{1,0:T(8,128)(2,1)} %param.9, bf16[1536,1536]{1,0:T(8,128)(2,1)} %all-gather.3.cloned.1.call-done), kind=kOutput, calls=%fused_computation | convolution fusion | flops 6041763840 | bytes 12582912 | tf_op jit(solution)/shard_map/dot_general | solution.py:28
  (119 shorter events, 47.2 us)
Async XLA Ops:
  7.2 705.3 %all-gather.3.cloned.1.call-start = ((), (), s32[]{:S(2)}) async-start(), calls=%async_computation.1 | async-start | bytes 5308416 | tf_op jit(solution)/shard_map/all_gather | solution.py:30
  418.1 19.0 %collective-permute-start.10 = (bf16[16,1536]{1,0:T(8,128)(2,1)S(1)}, bf16[16,1536]{1,0:T(8,128)(2,1)S(1)}, u32[]{:S(2)}, u32[]{:S(2)}) collective-permute-start(bf16[16,1536]{1,0:T(8,128)(2,1)S(1)} %convert.62), channel_id=1, source_target_pairs={{0,11},{1,12},{2,13},{3,14},{4,15},{5,16},{6,17},{7,18},{8,19},{9,... | collective-permute-start | bytes 147464
  419.4 19.1 %collective-permute-start.11 = (bf16[16,1536]{1,0:T(8,128)(2,1)S(1)}, bf16[16,1536]{1,0:T(8,128)(2,1)S(1)}, u32[]{:S(2)}, u32[]{:S(2)}) collective-permute-start(bf16[16,1536]{1,0:T(8,128)(2,1)S(1)} %convert.62), channel_id=1, source_target_pairs={{0,12},{1,13},{2,14},{3,15},{4,16},{5,17},{6,18},{7,19},{8,20},{9,... | collective-permute-start | bytes 147464
  420.7 25.8 %collective-permute-start.12 = (bf16[16,1536]{1,0:T(8,128)(2,1)S(1)}, bf16[16,1536]{1,0:T(8,128)(2,1)S(1)}, u32[]{:S(2)}, u32[]{:S(2)}) collective-permute-start(bf16[16,1536]{1,0:T(8,128)(2,1)S(1)} %convert.62), channel_id=1, source_target_pairs={{0,13},{1,14},{2,15},{3,16},{4,17},{5,18},{6,19},{7,20},{8,21},{9,... | collective-permute-start | bytes 147464
  422.0 31.7 %collective-permute-start.13 = (bf16[16,1536]{1,0:T(8,128)(2,1)S(1)}, bf16[16,1536]{1,0:T(8,128)(2,1)S(1)}, u32[]{:S(2)}, u32[]{:S(2)}) collective-permute-start(bf16[16,1536]{1,0:T(8,128)(2,1)S(1)} %convert.62), channel_id=1, source_target_pairs={{0,14},{1,15},{2,16},{3,17},{4,18},{5,19},{6,20},{7,21},{8,22},{9,... | collective-permute-start | bytes 147464
  425.0 32.7 %collective-permute-start.14 = (bf16[16,1536]{1,0:T(8,128)(2,1)S(1)}, bf16[16,1536]{1,0:T(8,128)(2,1)S(1)}, u32[]{:S(2)}, u32[]{:S(2)}) collective-permute-start(bf16[16,1536]{1,0:T(8,128)(2,1)S(1)} %convert.62), channel_id=1, source_target_pairs={{0,15},{1,16},{2,17},{3,18},{4,19},{5,20},{6,21},{7,22},{8,23},{9,... | collective-permute-start | bytes 147464
  437.1 21.9 %collective-permute-start.15 = (bf16[16,1536]{1,0:T(8,128)(2,1)S(1)}, bf16[16,1536]{1,0:T(8,128)(2,1)S(1)}, u32[]{:S(2)}, u32[]{:S(2)}) collective-permute-start(bf16[16,1536]{1,0:T(8,128)(2,1)S(1)} %convert.62), channel_id=1, source_target_pairs={{0,16},{1,17},{2,18},{3,19},{4,20},{5,21},{6,22},{7,23},{8,24},{9,... | collective-permute-start | bytes 147464
  438.4 22.9 %collective-permute-start.16 = (bf16[16,1536]{1,0:T(8,128)(2,1)S(1)}, bf16[16,1536]{1,0:T(8,128)(2,1)S(1)}, u32[]{:S(2)}, u32[]{:S(2)}) collective-permute-start(bf16[16,1536]{1,0:T(8,128)(2,1)S(1)} %convert.62), channel_id=1, source_target_pairs={{0,17},{1,18},{2,19},{3,20},{4,21},{5,22},{6,23},{7,24},{8,25},{9,... | collective-permute-start | bytes 147464
  446.4 18.0 %collective-permute-start.17 = (bf16[16,1536]{1,0:T(8,128)(2,1)S(1)}, bf16[16,1536]{1,0:T(8,128)(2,1)S(1)}, u32[]{:S(2)}, u32[]{:S(2)}) collective-permute-start(bf16[16,1536]{1,0:T(8,128)(2,1)S(1)} %convert.62), channel_id=1, source_target_pairs={{0,18},{1,19},{2,20},{3,21},{4,22},{5,23},{6,24},{7,25},{8,26},{9,... | collective-permute-start | bytes 147464
  453.7 14.5 %collective-permute-start.18 = (bf16[16,1536]{1,0:T(8,128)(2,1)S(1)}, bf16[16,1536]{1,0:T(8,128)(2,1)S(1)}, u32[]{:S(2)}, u32[]{:S(2)}) collective-permute-start(bf16[16,1536]{1,0:T(8,128)(2,1)S(1)} %convert.62), channel_id=1, source_target_pairs={{0,19},{1,20},{2,21},{3,22},{4,23},{5,24},{6,25},{7,26},{8,27},{9,... | collective-permute-start | bytes 147464
  457.7 11.8 %collective-permute-start.19 = (bf16[16,1536]{1,0:T(8,128)(2,1)S(1)}, bf16[16,1536]{1,0:T(8,128)(2,1)S(1)}, u32[]{:S(2)}, u32[]{:S(2)}) collective-permute-start(bf16[16,1536]{1,0:T(8,128)(2,1)S(1)} %convert.62), channel_id=1, source_target_pairs={{0,20},{1,21},{2,22},{3,23},{4,24},{5,25},{6,26},{7,27},{8,28},{9,... | collective-permute-start | bytes 147464
  459.0 12.4 %collective-permute-start.2 = (bf16[16,1536]{1,0:T(8,128)(2,1)S(1)}, bf16[16,1536]{1,0:T(8,128)(2,1)S(1)}, u32[]{:S(2)}, u32[]{:S(2)}) collective-permute-start(bf16[16,1536]{1,0:T(8,128)(2,1)S(1)} %convert.62), channel_id=1, source_target_pairs={{0,3},{1,4},{2,5},{3,6},{4,7},{5,8},{6,9},{7,10},{8,11},{9,12},{10... | collective-permute-start | bytes 147464
  461.3 12.1 %collective-permute-start.20 = (bf16[16,1536]{1,0:T(8,128)(2,1)S(1)}, bf16[16,1536]{1,0:T(8,128)(2,1)S(1)}, u32[]{:S(2)}, u32[]{:S(2)}) collective-permute-start(bf16[16,1536]{1,0:T(8,128)(2,1)S(1)} %convert.62), channel_id=1, source_target_pairs={{0,21},{1,22},{2,23},{3,24},{4,25},{5,26},{6,27},{7,28},{8,29},{9,... | collective-permute-start | bytes 147464
  464.4 11.6 %collective-permute-start.21 = (bf16[16,1536]{1,0:T(8,128)(2,1)S(1)}, bf16[16,1536]{1,0:T(8,128)(2,1)S(1)}, u32[]{:S(2)}, u32[]{:S(2)}) collective-permute-start(bf16[16,1536]{1,0:T(8,128)(2,1)S(1)} %convert.62), channel_id=1, source_target_pairs={{0,22},{1,23},{2,24},{3,25},{4,26},{5,27},{6,28},{7,29},{8,30},{9,... | collective-permute-start | bytes 147464
  471.5 11.6 %collective-permute-start.24 = (bf16[16,1536]{1,0:T(8,128)(2,1)S(1)}, bf16[16,1536]{1,0:T(8,128)(2,1)S(1)}, u32[]{:S(2)}, u32[]{:S(2)}) collective-permute-start(bf16[16,1536]{1,0:T(8,128)(2,1)S(1)} %convert.62), channel_id=1, source_target_pairs={{0,25},{1,26},{2,27},{3,28},{4,29},{5,30},{6,31},{7,32},{8,33},{9,... | collective-permute-start | bytes 147464
  476.0 12.6 %collective-permute-start.26 = (bf16[16,1536]{1,0:T(8,128)(2,1)S(1)}, bf16[16,1536]{1,0:T(8,128)(2,1)S(1)}, u32[]{:S(2)}, u32[]{:S(2)}) collective-permute-start(bf16[16,1536]{1,0:T(8,128)(2,1)S(1)} %convert.62), channel_id=1, source_target_pairs={{0,27},{1,28},{2,29},{3,30},{4,31},{5,32},{6,33},{7,34},{8,35},{9,... | collective-permute-start | bytes 147464
  477.6 12.9 %collective-permute-start.27 = (bf16[16,1536]{1,0:T(8,128)(2,1)S(1)}, bf16[16,1536]{1,0:T(8,128)(2,1)S(1)}, u32[]{:S(2)}, u32[]{:S(2)}) collective-permute-start(bf16[16,1536]{1,0:T(8,128)(2,1)S(1)} %convert.62), channel_id=1, source_target_pairs={{0,28},{1,29},{2,30},{3,31},{4,32},{5,33},{6,34},{7,35},{8,36},{9,... | collective-permute-start | bytes 147464
  479.9 13.0 %collective-permute-start.28 = (bf16[16,1536]{1,0:T(8,128)(2,1)S(1)}, bf16[16,1536]{1,0:T(8,128)(2,1)S(1)}, u32[]{:S(2)}, u32[]{:S(2)}) collective-permute-start(bf16[16,1536]{1,0:T(8,128)(2,1)S(1)} %convert.62), channel_id=1, source_target_pairs={{0,29},{1,30},{2,31},{3,32},{4,33},{5,34},{6,35},{7,36},{8,37},{9,... | collective-permute-start | bytes 147464
  484.4 13.0 %collective-permute-start.3 = (bf16[16,1536]{1,0:T(8,128)(2,1)S(1)}, bf16[16,1536]{1,0:T(8,128)(2,1)S(1)}, u32[]{:S(2)}, u32[]{:S(2)}) collective-permute-start(bf16[16,1536]{1,0:T(8,128)(2,1)S(1)} %convert.62), channel_id=1, source_target_pairs={{0,4},{1,5},{2,6},{3,7},{4,8},{5,9},{6,10},{7,11},{8,12},{9,13},{1... | collective-permute-start | bytes 147464
  488.6 13.2 %collective-permute-start.30 = (bf16[16,1536]{1,0:T(8,128)(2,1)S(1)}, bf16[16,1536]{1,0:T(8,128)(2,1)S(1)}, u32[]{:S(2)}, u32[]{:S(2)}) collective-permute-start(bf16[16,1536]{1,0:T(8,128)(2,1)S(1)} %convert.62), channel_id=1, source_target_pairs={{0,31},{1,32},{2,33},{3,34},{4,35},{5,36},{6,37},{7,38},{8,39},{9,... | collective-permute-start | bytes 147464
  490.5 12.8 %collective-permute-start.4 = (bf16[16,1536]{1,0:T(8,128)(2,1)S(1)}, bf16[16,1536]{1,0:T(8,128)(2,1)S(1)}, u32[]{:S(2)}, u32[]{:S(2)}) collective-permute-start(bf16[16,1536]{1,0:T(8,128)(2,1)S(1)} %convert.62), channel_id=1, source_target_pairs={{0,5},{1,6},{2,7},{3,8},{4,9},{5,10},{6,11},{7,12},{8,13},{9,14},{... | collective-permute-start | bytes 147464
  492.9 13.9 %collective-permute-start.5 = (bf16[16,1536]{1,0:T(8,128)(2,1)S(1)}, bf16[16,1536]{1,0:T(8,128)(2,1)S(1)}, u32[]{:S(2)}, u32[]{:S(2)}) collective-permute-start(bf16[16,1536]{1,0:T(8,128)(2,1)S(1)} %convert.62), channel_id=1, source_target_pairs={{0,6},{1,7},{2,8},{3,9},{4,10},{5,11},{6,12},{7,13},{8,14},{9,15},... | collective-permute-start | bytes 147464
  494.5 12.3 %collective-permute-start.6 = (bf16[16,1536]{1,0:T(8,128)(2,1)S(1)}, bf16[16,1536]{1,0:T(8,128)(2,1)S(1)}, u32[]{:S(2)}, u32[]{:S(2)}) collective-permute-start(bf16[16,1536]{1,0:T(8,128)(2,1)S(1)} %convert.62), channel_id=1, source_target_pairs={{0,7},{1,8},{2,9},{3,10},{4,11},{5,12},{6,13},{7,14},{8,15},{9,16}... | collective-permute-start | bytes 147464
  565.0 85.1 %all-to-all-start = ((bf16[8,192,1536]{2,1,0:T(8,128)(2,1)}), bf16[8,192,1536]{2,1,0:T(8,128)(2,1)}, u32[]{:S(2)}, u32[]{:S(2)}) async-start(bf16[8,192,1536]{2,1,0:T(8,128)(2,1)} %stack.2), calls=%async_computation | async-start | bytes 9437184 | tf_op jit(solution)/shard_map/all_to_all | solution.py:24
  (38 other events, 1395.8 us)
Sparse Core Ops, SparseCore 0:
  562.5 149.8 all-gather.2
